TPU v7x, 512 devices: a whole 4x8x8 slice. The times are simulated.
512 devices in a mesh: pipe: 64 (over z, y_hi, core), tensor: 8 (over y_lo, x).
Axes of the slice: x: 4, y: 8 (y_hi: 4, y_lo: 2; y = y_hi * 2 + y_lo), z: 8, core: 2. Of those that a mesh axis runs over, the one named last changes fastest.
Arguments:
- qkv_now: bfloat16 [64, 3, 128, 6144], P('pipe', None, None, 'tensor'), may hold values from -150 to 150
- held_stash: bfloat16 [64, 2, 3, 128, 6144], P('pipe', None, None, None, 'tensor'), may hold values from -150 to 150
- cotangent: bfloat16 [64, 128, 6144], P('pipe', None, 'tensor'), may hold values from -6 to 6
- norm_gain: float32 [6144], P('tensor'), may hold values from 0.1 to 1.9
- fetch_slot: int32 [64], replicated, may hold values from 0 to 1
Outputs:
- forward_in: bfloat16 [64, 128, 6144], P('pipe', None, 'tensor')
- grads_in: bfloat16 [64, 3, 128, 6144], P('pipe', None, None, 'tensor')
- evicted: bfloat16 [64, 128, 6144], P('pipe', None, 'tensor')
All inputs are finite; a program needn't handle non-finite values.
Results may differ from a plain program's by a relative error of at most 0.009.
Values may be sent and summed in bfloat16 or wider, within the bound.
A program may use at most 64 MiB of HBM per device.

v0:
```python
import jax
import jax.numpy as jnp
from jax import lax
from jax.sharding import PartitionSpec as P

HS = 128


EPS = 1e-05


def shifted(x, axis, by):
    length = lax.axis_size(axis)
    pairs = [(i, i + by) for i in range(length) if 0 <= i + by < length]
    return lax.ppermute(x, axis, pairs)


def attend_heads(queries, keys_in, values_in):
    rows, width = queries.shape
    heads = width // HS
    query_heads = queries.reshape(rows, heads, HS)
    key_heads = keys_in.reshape(rows, heads, HS)
    value_heads = values_in.reshape(rows, heads, HS)
    score_scale = HS ** (-0.5)
    scores = (
        jnp.einsum("ihd,jhd->hij", query_heads, key_heads, preferred_element_type=jnp.float32)
        * score_scale
    )
    causal = jnp.arange(rows)[:, None] >= jnp.arange(rows)[None, :]
    masked = jnp.where(causal[None], scores, -1e30)
    maxima = jnp.max(masked, axis=-1, keepdims=True)
    expo = jnp.exp(masked - maxima)
    probabilities = expo / jnp.sum(expo, axis=-1, keepdims=True)
    prob_bf16 = probabilities.astype(jnp.bfloat16)
    attended = jnp.einsum(
        "hij,jhd->ihd", prob_bf16, value_heads, preferred_element_type=jnp.float32
    )
    return (attended.reshape(rows, width).astype(jnp.bfloat16), probabilities, prob_bf16)


def attend_backward(triple, probabilities, prob_bf16, d_out):
    rows, width = d_out.shape
    heads = width // HS
    d_heads = d_out.reshape(rows, heads, HS)
    query_heads = triple[0].reshape(rows, heads, HS)
    key_heads = triple[1].reshape(rows, heads, HS)
    value_heads = triple[2].reshape(rows, heads, HS)
    d_values = jnp.einsum("hij,ihd->jhd", prob_bf16, d_heads, preferred_element_type=jnp.float32)
    d_probs = jnp.einsum("ihd,jhd->hij", d_heads, value_heads, preferred_element_type=jnp.float32)
    delta = jnp.sum(probabilities * d_probs, axis=-1, keepdims=True)
    d_scores = (probabilities * (d_probs - delta) * HS ** (-0.5)).astype(jnp.bfloat16)
    d_queries = jnp.einsum("hij,jhd->ihd", d_scores, key_heads, preferred_element_type=jnp.float32)
    d_keys = jnp.einsum("hij,ihd->jhd", d_scores, query_heads, preferred_element_type=jnp.float32)
    return jnp.stack(
        [d_queries.reshape(rows, width), d_keys.reshape(rows, width), d_values.reshape(rows, width)]
    ).astype(jnp.bfloat16)


def shards(qkv_now, held_stash, cotangent, norm_gain, fetch_slot):
    section_count = lax.axis_size("pipe")
    my_section = lax.axis_index("pipe")
    current = qkv_now[0]
    rows, width = (current.shape[1], current.shape[2])
    attended, unused_p, unused_b = attend_heads(current[0], current[1], current[2])
    held_slots = held_stash[0]
    payload = jnp.concatenate([held_slots.reshape(-1, rows, width), attended[None]], axis=0)
    payload_shape = payload.shape
    blocks = payload.reshape(section_count, -1)
    spread = lax.all_to_all(blocks, "pipe", split_axis=0, concat_axis=0, tiled=True)
    turned = spread[::-1]
    returned = lax.all_to_all(turned, "pipe", split_axis=0, concat_axis=0, tiled=True)
    payload = returned.reshape(payload_shape)
    fetched = lax.dynamic_slice_in_dim(payload, fetch_slot[my_section] * 3, 3, 0)
    evicted = payload[-1]
    back_out, probabilities, prob_bf16 = attend_heads(fetched[0], fetched[1], fetched[2])
    features_total = width * lax.axis_size("tensor")
    att_f = attended.astype(jnp.float32)
    back_f = back_out.astype(jnp.float32)
    gain_row = norm_gain[None, :]
    scaled_cot = gain_row * cotangent[0].astype(jnp.float32)
    square_now, square_back, dot_rows = lax.psum(
        (
            jnp.sum(att_f * att_f, axis=-1),
            jnp.sum(back_f * back_f, axis=-1),
            jnp.sum(scaled_cot * back_f, axis=-1),
        ),
        "tensor",
    )
    ratio = lax.rsqrt(square_now / features_total + EPS)
    normed = (att_f * ratio[:, None] * gain_row).astype(jnp.bfloat16)
    back_ratio = lax.rsqrt(square_back / features_total + EPS)
    d_out = (
        back_ratio[:, None] * scaled_cot
        - back_f * (back_ratio**3 * dot_rows / features_total)[:, None]
    ).astype(jnp.bfloat16)
    grads = attend_backward(fetched, probabilities, prob_bf16, d_out)
    forward_in = shifted(normed[None], "pipe", 1)
    grads_in = shifted(grads[None], "pipe", -1)
    return (forward_in, grads_in, evicted[None])


def solution(mesh):
    return jax.shard_map(
        shards,
        mesh=mesh,
        in_specs=(
            P("pipe", None, None, "tensor"),
            P("pipe", None, None, None, "tensor"),
            P("pipe", None, "tensor"),
            P("tensor"),
            P(),
        ),
        out_specs=(
            P("pipe", None, "tensor"),
            P("pipe", None, None, "tensor"),
            P("pipe", None, "tensor"),
        ),
        check_vma=False,
    )
```

profile of v0, /device:TPU:129, one launch (start us, length us, event | category | flops | bytes accessed | tf_op | source)
XLA Modules:
  0.0 237.6 jit_solution(5885420402752708146)
XLA Ops:
  0.7 1.2 fusion.34
  1.8 0.2 copy.101
  2.0 0.2 copy.135
  2.1 0.2 copy.136
  2.3 0.3 fusion.8
  2.7 0.8 multiply_reduce_fusion.2
  3.7 0.2 copy-done
  3.9 1.2 pad_maximum_fusion
  5.1 4.1 %all_to_all.19 = bf16[64,1,10752]{2,1,0:T(2,128)(2,1)S(1)} reshape(bf16[7,128,768]{2,1,0:T(8,128)(2,1)} %pad_maximum_fusion) | data formatting | bytes 2752512 | tf_op jit(solution)/shard_map/all_to_all | solution.py:69
  9.2 0.5 broadcast.96
  9.7 10.1 %reduce.5 = bf16[64,10752]{1,0:T(8,128)(2,1)} reduce(bf16[64,1,10752]{2,1,0:T(2,128)(2,1)S(1)} %all_to_all.19, bf16[]{:T(256)} %broadcast.96), dimensions={1}, to_apply=%all_to_all.19.reduce_sub_computation | reduce | bytes 2752514 | tf_op jit(solution)/shard_map/all_to_all | solution.py:69
  19.7 1.5 reshape.188
  21.2 55.3 %all_to_all.22 = bf16[64,2,5376]{2,1,0:T(2,128)(2,1)} all-to-all(bf16[64,2,5376]{2,1,0:T(2,128)(2,1)S(1)} %reshape.188), channel_id=1, replica_groups=mesh['pipe'=64,'tensor'=8] {'pipe'}, dimensions={0} | all-to-all | bytes 2752512 | tf_op jit(solution)/shard_map/all_to_all | solution.py:69
  76.5 7.7 %reshape.189 = bf16[64,1,10752]{2,1,0:T(2,128)(2,1)S(1)} reshape(bf16[64,2,5376]{2,1,0:T(2,128)(2,1)} %all_to_all.22) | data formatting | bytes 2752512
  84.3 1.2 copy.138
  85.5 30.9 %rev.3 = bf16[64,10752]{1,0:T(8,128)(2,1)S(1)} reverse(bf16[64,10752]{1,0:T(8,128)(2,1)} %bitcast.56), dimensions={0} | reverse | bytes 2752512 | tf_op jit(solution)/shard_map/rev | solution.py:70
  116.5 1.7 reduce.6
  118.2 1.3 reshape.190
  119.5 10.9 %all-to-all-start.1 = ((bf16[64,2,5376]{2,1,0:T(2,128)(2,1)}), bf16[64,2,5376]{2,1,0:T(2,128)(2,1)}, u32[]{:S(2)}, u32[]{:S(2)}) async-start(bf16[64,2,5376]{2,1,0:T(2,128)(2,1)} %reshape.190), calls=%async_computation.1 | async-start | bytes 2752512 | tf_op jit(solution)/shard_map/all_to_all | solution.py:71
  130.4 0.6 dynamic_slice.6
  131.8 31.4 %all-to-all-done.1 = bf16[64,2,5376]{2,1,0:T(2,128)(2,1)} async-done(((bf16[64,2,5376]{2,1,0:T(2,128)(2,1)}), bf16[64,2,5376]{2,1,0:T(2,128)(2,1)}, u32[]{:S(2)}, u32[]{:S(2)}) %all-to-all-start.1) | async-done | bytes 1376288 | tf_op jit(solution)/shard_map/all_to_all | solution.py:71
  163.2 7.7 %reshape.191 = bf16[64,1,10752]{2,1,0:T(2,128)(2,1)S(1)} reshape(bf16[64,2,5376]{2,1,0:T(2,128)(2,1)} %all-to-all-done.1) | data formatting | bytes 2752512
  171.0 9.4 %reduce.4 = bf16[64,10752]{1,0:T(8,128)(2,1)} reduce(bf16[64,1,10752]{2,1,0:T(2,128)(2,1)S(1)} %reshape.191, bf16[]{:T(256)} %constant.33), dimensions={1}, to_apply=%all_to_all.18.reduce_sub_computation | reduce | bytes 2752514 | tf_op jit(solution)/shard_map/all_to_all | solution.py:71
  180.4 3.3 %reshape.183 = bf16[7,128,768]{2,1,0:T(8,128)(2,1)S(1)} reshape(bf16[64,10752]{1,0:T(8,128)(2,1)} %reduce.4) | data formatting | bytes 2752512 | tf_op jit(solution)/shard_map/reshape | solution.py:72
  183.7 0.7 fusion.33
  184.4 0.2 copy.111
  184.6 0.2 copy.108
  184.7 0.2 copy.107
  184.9 0.3 fusion.9
  185.2 0.4 fusion.36
  185.6 0.3 multiply_reduce_fusion.1
  185.9 0.2 copy.114
  186.0 0.2 copy-done.2
  186.4 13.7 %all-reduce = (f32[128]{0:T(128)S(1)}, f32[128]{0:T(128)S(1)}, f32[128]{0:T(128)S(1)}) all-reduce(f32[128]{0:T(128)S(1)} %copy-done.4, f32[128]{0:T(128)S(1)} %fusion.20, f32[128]{0:T(128)S(1)} %get-tuple-element.22), channel_id=1, replica_groups=mesh['pipe'=64,'tensor'=8] {'tensor'}, use_global_device_ids=true, to_apply=%region_3.4 | all-reduce | flops 384 | bytes 3072 | tf_op jit(solution)/shard_map/psum | solution.py:81
  200.1 0.2 fusion.18
  200.3 0.3 convolution_convert_fusion.1
  200.6 0.3 fusion.37
  200.9 0.3 convolution_convert_fusion.2
  201.2 0.3 convolution_convert_fusion.3
  201.4 0.1 copy.122
  201.6 0.1 copy.121
  201.7 0.1 copy.120
  202.0 7.6 %collective-permute-start.1 = (bf16[1,3,128,768]{3,2,1,0:T(8,128)(2,1)S(1)}, bf16[1,3,128,768]{3,2,1,0:T(8,128)(2,1)S(1)}, u32[]{:S(2)}, u32[]{:S(2)}) collective-permute-start(bf16[1,3,128,768]{3,2,1,0:T(8,128)(2,1)S(1)} %pad_maximum_fusion.1), channel_id=1, source_target_pairs={{8,0},{16,8},{24,16},{32,24},{40,32},{48,40},{56,48},{64,56},{72,6... | collective-permute-start | bytes 1769480 | tf_op jit(solution)/shard_map/ppermute | solution.py:15
  209.7 15.2 %collective-permute-start = (bf16[1,128,768]{2,1,0:T(8,128)(2,1)S(1)}, bf16[1,128,768]{2,1,0:T(8,128)(2,1)S(1)}, u32[]{:S(2)}, u32[]{:S(2)}) collective-permute-start(bf16[1,128,768]{2,1,0:T(8,128)(2,1)S(1)} %multiply_convert_fusion), channel_id=1, source_target_pairs={{0,8},{8,16},{16,24},{24,32},{32,40},{40,48},{48,56},{56,64},{64,7... | collective-permute-start | bytes 589832 | tf_op jit(solution)/shard_map/ppermute | solution.py:15
  224.9 4.0 %collective-permute-done = bf16[1,128,768]{2,1,0:T(8,128)(2,1)S(1)} collective-permute-done((bf16[1,128,768]{2,1,0:T(8,128)(2,1)S(1)}, bf16[1,128,768]{2,1,0:T(8,128)(2,1)S(1)}, u32[]{:S(2)}, u32[]{:S(2)}) %collective-permute-start) | collective-permute-done | bytes 196640 | tf_op jit(solution)/shard_map/ppermute | solution.py:15
  228.9 7.2 %collective-permute-done.1 = bf16[1,3,128,768]{3,2,1,0:T(8,128)(2,1)S(1)} collective-permute-done((bf16[1,3,128,768]{3,2,1,0:T(8,128)(2,1)S(1)}, bf16[1,3,128,768]{3,2,1,0:T(8,128)(2,1)S(1)}, u32[]{:S(2)}, u32[]{:S(2)}) %collective-permute-start.1) | collective-permute-done | bytes 589856 | tf_op jit(solution)/shard_map/ppermute | solution.py:15
  236.1 0.7 copy.142
  236.8 0.8 copy.143
  (17 shorter events, 0.7 us)
Async XLA Ops:
  2.6 1.3 copy-start
  119.5 11.0 %copy-start.3 = (s32[64]{0:T(128)S(1)}, s32[64]{0:T(128)}, u32[]{:S(2)}) copy-start(s32[64]{0:T(128)} %param.9) | copy-start | bytes 772
  119.5 12.2 %copy-start.1 = (bf16[1,128,768]{2,1,0:T(8,128)(2,1)S(1)}, bf16[1,128,768]{2,1,0:T(8,128)(2,1)}, u32[]{:S(2)}) copy-start(bf16[1,128,768]{2,1,0:T(8,128)(2,1)} %param.7) | copy-start | bytes 589828
  119.5 43.7 %all-to-all-start.1 = ((bf16[64,2,5376]{2,1,0:T(2,128)(2,1)}), bf16[64,2,5376]{2,1,0:T(2,128)(2,1)}, u32[]{:S(2)}, u32[]{:S(2)}) async-start(bf16[64,2,5376]{2,1,0:T(2,128)(2,1)} %reshape.190), calls=%async_computation.1 | async-start | bytes 2752512 | tf_op jit(solution)/shard_map/all_to_all | solution.py:71
  185.5 0.7 copy-start.2
  185.5 0.8 copy-start.4
  202.0 34.2 %collective-permute-start.1 = (bf16[1,3,128,768]{3,2,1,0:T(8,128)(2,1)S(1)}, bf16[1,3,128,768]{3,2,1,0:T(8,128)(2,1)S(1)}, u32[]{:S(2)}, u32[]{:S(2)}) collective-permute-start(bf16[1,3,128,768]{3,2,1,0:T(8,128)(2,1)S(1)} %pad_maximum_fusion.1), channel_id=1, source_target_pairs={{8,0},{16,8},{24,16},{32,24},{40,32},{48,40},{56,48},{64,56},{72,6... | collective-permute-start | bytes 1769480 | tf_op jit(solution)/shard_map/ppermute | solution.py:15
  209.7 19.3 %collective-permute-start = (bf16[1,128,768]{2,1,0:T(8,128)(2,1)S(1)}, bf16[1,128,768]{2,1,0:T(8,128)(2,1)S(1)}, u32[]{:S(2)}, u32[]{:S(2)}) collective-permute-start(bf16[1,128,768]{2,1,0:T(8,128)(2,1)S(1)} %multiply_convert_fusion), channel_id=1, source_target_pairs={{0,8},{8,16},{16,24},{24,32},{32,40},{40,48},{48,56},{56,64},{64,7... | collective-permute-start | bytes 589832 | tf_op jit(solution)/shard_map/ppermute | solution.py:15
where the time goes:
time: 241 us; the launch traced here: 238 us
  blocking collectives  69.1 us (29%)
  local copies, waits for them, and re-layouts  64.6 us (27%)
  waiting for transfers between devices  42.6 us (18%)
  starting transfers between devices  33.7 us (14%)
  other arithmetic  23.4 us (10%)
  matrix products  2.73 us (1%)
    all_to_all x1, blocking collectives, shards(): lax.all_to_all(blocks, 'pipe', split_axis=0, concat_axis=0, tiled=True)  55.3 us
    all_to_all x1, waiting for transfers between devices, shards(): lax.all_to_all(turned, 'pipe', split_axis=0, concat_axis=0, tiled=True)  31.4 us
    rev x1, local copies, waits for them, and re-layouts, shards(): turned = spread[::-1]  30.9 us
    ppermute x2, starting transfers between devices, shifted(): return lax.ppermute(x, axis, pairs)  22.8 us
    unnamed x19, local copies, waits for them, and re-layouts  21.7 us
    psum x1, blocking collectives, shards(): lax.psum((jnp.sum(att_f * att_f, axis=-1), jnp.sum(back_f * back_f, axis=...  13.7 us
    ppermute x2, waiting for transfers between devices, shifted(): return lax.ppermute(x, axis, pairs)  11.2 us
    all_to_all x2, other arithmetic, shards(): lax.all_to_all(turned, 'pipe', split_axis=0, concat_axis=0, tiled=True)  11.1 us
  transfers between devices with their start and end apart: 3, of which 3 were waited for; matrix products, arithmetic and copies ran while one was open for 0% of the time, Pallas kernels for 0%

commit v1 on v0

v1 whole, which is shorter than its diff:
```python
import functools

import jax
import jax.numpy as jnp
from jax import lax
from jax.experimental import pallas as pl
from jax.experimental.pallas import tpu as pltpu
from jax.sharding import PartitionSpec as P

MESH = pl.DeviceIdType.MESH
HS = 128
EPS = 1e-05
F32 = jnp.float32
BF16 = jnp.bfloat16


def dot(x, y, dims):
    return lax.dot_general(x, y, (dims, ((), ())), preferred_element_type=F32)


def softmax_rows(queries, keys, causal):
    scores = dot(queries, keys, ((1,), (1,))) * HS ** (-0.5)
    masked = jnp.where(causal, scores, -1e30)
    expo = jnp.exp(masked - jnp.max(masked, axis=-1, keepdims=True))
    return expo / jnp.sum(expo, axis=-1, keepdims=True)


def as_row(partial):
    return jnp.sum(partial.T, axis=0, keepdims=True)


def as_columns(row):
    return jnp.broadcast_to(row, (HS, row.shape[1])).T


def kernel(
    sections, members, heads, feats,
    qkv_ref, held_ref, cot_ref, gain_ref, slot_ref,
    fwd_ref, grads_ref, evict_ref,
    held_v, send_v, back_v, qkv_v, cot_v, att_v, norm_v, prob_v, pb_v, ob_v, grad_v,
    sum_v, sums_now, sums_back,
    held_sem, qkv_sem, self_sem, zero_sem, grad_sem,
    stash_send, stash_recv, cot_send, cot_recv, evict_send, evict_recv, fwd_send, fwd_recv,
    now_send, now_recv, bsum_send, bsum_recv,
):
    p = lax.axis_index("pipe")
    t = lax.axis_index("tensor")
    last = sections - 1
    mirror = last - p
    target = last - 1 - p
    has_up = p < last
    has_down = p > 0
    to_self = target == p
    paired = has_up & jnp.logical_not(to_self)

    loads = []
    for h in range(heads):
        loads.append(pltpu.make_async_copy(held_ref.at[0, :, :, :, pl.ds(h * HS, HS)], held_v.at[h], held_sem.at[h]))
        loads[h].start()
    qkv_load = pltpu.make_async_copy(qkv_ref.at[0], qkv_v, qkv_sem)
    qkv_load.start()

    barrier = pltpu.get_barrier_semaphore()

    def greet(section, member):
        pl.semaphore_signal(barrier, inc=1, device_id=(section, member), device_id_type=MESH)

    greet(mirror, t)
    pl.when(paired)(lambda: greet(target, t))
    pl.when(has_up)(lambda: greet(p + 1, t))
    pl.when(has_down)(lambda: greet(p - 1, t))
    for d in range(1, members):
        greet(p, lax.rem(t + d, members))

    def one(flag):
        return jnp.where(flag, 1, 0)

    stash = [
        pltpu.make_async_remote_copy(
            src_ref=send_v.at[h], dst_ref=back_v.at[h], send_sem=stash_send.at[h], recv_sem=stash_recv.at[h],
            device_id=(target, t), device_id_type=MESH,
        )
        for h in range(heads)
    ]
    cot_move = pltpu.make_async_remote_copy(
        src_ref=cot_ref.at[0], dst_ref=cot_v, send_sem=cot_send, recv_sem=cot_recv, device_id=(p - 1, t), device_id_type=MESH
    )
    evict_move = pltpu.make_async_remote_copy(
        src_ref=att_v, dst_ref=evict_ref.at[0], send_sem=evict_send, recv_sem=evict_recv, device_id=(mirror, t), device_id_type=MESH
    )
    fwd_move = pltpu.make_async_remote_copy(
        src_ref=norm_v, dst_ref=fwd_ref.at[0], send_sem=fwd_send, recv_sem=fwd_recv, device_id=(p + 1, t), device_id_type=MESH
    )

    def sum_moves(which, buffer, sends, recvs):
        return [
            pltpu.make_async_remote_copy(
                src_ref=sum_v.at[which], dst_ref=buffer.at[d - 1], send_sem=sends.at[d - 1], recv_sem=recvs.at[d - 1],
                device_id=(p, lax.rem(t + d, members)), device_id_type=MESH,
            )
            for d in range(1, members)
        ]

    slot = slot_ref[mirror]
    for h in range(heads):
        loads[h].wait()
        for i in range(3):
            send_v[h, i] = jnp.where(slot == 1, held_v[h, 1, i], held_v[h, 0, i])
        if h == 0:
            pl.semaphore_wait(barrier, members + one(paired) + one(has_up) + one(has_down))
        pl.when(paired)(stash[h].start)

    pl.when(has_down)(cot_move.start)

    @pl.when(to_self)
    def _():
        own = pltpu.make_async_copy(send_v, back_v, self_sem)
        own.start()
        own.wait()

    @pl.when(p == last)
    def _():
        back_v[...] = jnp.zeros_like(back_v)
        cot_v[...] = jnp.zeros_like(cot_v)

    rows = lax.broadcasted_iota(jnp.int32, (HS, HS), 0)
    causal = rows >= lax.broadcasted_iota(jnp.int32, (HS, HS), 1)
    qkv_load.wait()
    squares = jnp.zeros((HS, HS), F32)
    for h in range(heads):
        cols = pl.ds(h * HS, HS)
        probs = softmax_rows(qkv_v[0, :, cols], qkv_v[1, :, cols], causal)
        out = dot(probs.astype(BF16), qkv_v[2, :, cols], ((1,), (0,))).astype(BF16)
        att_v[:, cols] = out
        out = out.astype(F32)
        squares += out * out
    sum_v[0] = jnp.broadcast_to(as_row(squares), (8, HS))
    now_moves = sum_moves(0, sums_now, now_send, now_recv)
    for move in now_moves:
        move.start()
    for move in now_moves:
        move.wait_recv()
    total = sum_v[0, 0:1]
    for d in range(members - 1):
        total += sums_now[d, 0:1]
    ratio = as_columns(lax.rsqrt(total / feats + EPS))
    for h in range(heads):
        cols = pl.ds(h * HS, HS)
        norm_v[:, cols] = (att_v[:, cols].astype(F32) * ratio * gain_ref[:, cols]).astype(BF16)
    pl.when(has_up)(fwd_move.start)

    @pl.when(p == 0)
    def _():
        grad_v[0] = jnp.zeros_like(grad_v[0])
        zeros = pltpu.make_async_copy(grad_v.at[0], fwd_ref.at[0], zero_sem)
        zeros.start()
        zeros.wait()

    pl.when(has_up)(cot_move.wait_recv)
    squares = jnp.zeros((HS, HS), F32)
    dots = jnp.zeros((HS, HS), F32)
    for h in range(heads):
        cols = pl.ds(h * HS, HS)
        pl.when(paired)(stash[h].wait_send)
        if h == heads - 1:
            evict_move.start()
        pl.when(paired)(stash[h].wait_recv)
        probs = softmax_rows(back_v[h, 0], back_v[h, 1], causal)
        prob_v[h] = probs
        probs = probs.astype(BF16)
        pb_v[h] = probs
        out = dot(probs, back_v[h, 2], ((1,), (0,))).astype(BF16)
        ob_v[h] = out
        out = out.astype(F32)
        squares += out * out
        dots += gain_ref[:, cols] * cot_v[:, cols].astype(F32) * out
    sum_v[1] = jnp.concatenate([as_row(squares), as_row(dots), jnp.zeros((6, HS), F32)], axis=0)
    back_moves = sum_moves(1, sums_back, bsum_send, bsum_recv)
    for move in back_moves:
        move.start()
    for move in back_moves:
        move.wait_recv()
    total = sum_v[1]
    for d in range(members - 1):
        total += sums_back[d]
    back_ratio = lax.rsqrt(total[0:1] / feats + EPS)
    pull = as_columns(back_ratio**3 * total[1:2] / feats)
    back_ratio = as_columns(back_ratio)

    for h in range(heads):
        cols = pl.ds(h * HS, HS)
        scaled = gain_ref[:, cols] * cot_v[:, cols].astype(F32)
        d_out = (back_ratio * scaled - ob_v[h].astype(F32) * pull).astype(BF16)
        probs = prob_v[h]
        d_values = dot(pb_v[h], d_out, ((0,), (0,)))
        d_probs = dot(d_out, back_v[h, 2], ((1,), (1,)))
        delta = jnp.sum(probs * d_probs, axis=-1, keepdims=True)
        d_scores = (probs * (d_probs - delta) * HS ** (-0.5)).astype(BF16)
        grad_v[0, :, cols] = dot(d_scores, back_v[h, 1], ((1,), (0,))).astype(BF16)
        grad_v[1, :, cols] = dot(d_scores, back_v[h, 0], ((0,), (0,))).astype(BF16)
        grad_v[2, :, cols] = d_values.astype(BF16)
    grads_out = pltpu.make_async_copy(grad_v, grads_ref.at[0], grad_sem)
    grads_out.start()

    pl.when(has_down)(cot_move.wait_send)
    pl.when(has_up)(fwd_move.wait_send)
    pl.when(has_down)(fwd_move.wait_recv)
    for move in now_moves + back_moves:
        move.wait_send()
    grads_out.wait()
    evict_move.wait()


def shards(sections, members, qkv_now, held_stash, cotangent, norm_gain, fetch_slot):
    rows, width = cotangent.shape[1:]
    heads = width // HS
    anywhere = pl.BlockSpec(memory_space=pl.ANY)
    dma = pltpu.SemaphoreType.DMA
    return pl.pallas_call(
        functools.partial(kernel, sections, members, heads, float(width * members)),
        name="section_step",
        out_shape=(
            jax.ShapeDtypeStruct((1, rows, width), BF16),
            jax.ShapeDtypeStruct((1, 3, rows, width), BF16),
            jax.ShapeDtypeStruct((1, rows, width), BF16),
        ),
        in_specs=[
            anywhere, anywhere, anywhere,
            pl.BlockSpec(memory_space=pltpu.VMEM),
            pl.BlockSpec(memory_space=pltpu.SMEM),
        ],
        out_specs=(anywhere, anywhere, anywhere),
        scratch_shapes=[
            pltpu.VMEM((heads, 2, 3, rows, HS), BF16),
            pltpu.VMEM((heads, 3, rows, HS), BF16),
            pltpu.VMEM((heads, 3, rows, HS), BF16),
            pltpu.VMEM((3, rows, width), BF16),
            pltpu.VMEM((rows, width), BF16),
            pltpu.VMEM((rows, width), BF16),
            pltpu.VMEM((rows, width), BF16),
            pltpu.VMEM((heads, rows, rows), F32),
            pltpu.VMEM((heads, rows, rows), BF16),
            pltpu.VMEM((heads, rows, HS), BF16),
            pltpu.VMEM((3, rows, width), BF16),
            pltpu.VMEM((2, 8, rows), F32),
            pltpu.VMEM((members - 1, 8, rows), F32),
            pltpu.VMEM((members - 1, 8, rows), F32),
            dma((heads,)), dma, dma, dma, dma,
            dma((heads,)), dma((heads,)), dma, dma, dma, dma, dma, dma,
            dma((members - 1,)), dma((members - 1,)), dma((members - 1,)), dma((members - 1,)),
        ],
        compiler_params=pltpu.CompilerParams(
            collective_id=0, has_side_effects=True, vmem_limit_bytes=24 * 1024 * 1024
        ),
    )(qkv_now, held_stash, cotangent, norm_gain[None, :], fetch_slot)


def solution(mesh):
    return jax.shard_map(
        functools.partial(shards, mesh.shape["pipe"], mesh.shape["tensor"]),
        mesh=mesh,
        in_specs=(
            P("pipe", None, None, "tensor"),
            P("pipe", None, None, None, "tensor"),
            P("pipe", None, "tensor"),
            P("tensor"),
            P(),
        ),
        out_specs=(
            P("pipe", None, "tensor"),
            P("pipe", None, None, "tensor"),
            P("pipe", None, "tensor"),
        ),
        check_vma=False,
    )
```

time: 241 us -> 67.3 us (0.28)
  the two profiles are of different devices: /device:TPU:129 before, /device:TPU:57 now
where the time goes in v1:
time: 67.3 us; the launch traced here: 67 us
  Pallas kernels  59.6 us (89%)
  local copies, waits for them, and re-layouts  6.78 us (10%)
    pallas_call x1, Pallas kernels, shards(): pl.pallas_call(functools.partial(kernel, sections, members, heads, float(...  59.6 us
    unnamed x11, local copies, waits for them, and re-layouts  6.08 us

profile of v1, /device:TPU:57, one launch (start us, length us, event | category | flops | bytes accessed | tf_op | source)
XLA Modules:
  0.0 67.0 jit_solution(6649684343970170903)
XLA Ops:
  0.6 0.7 %broadcast_in_dim.3.gain_ref = f32[1,768]{1,0:T(1,128)S(1)} reshape(f32[768]{0:T(1024)} %param.8) | data formatting | bytes 6144 | tf_op jit(solution)/shard_map/broadcast_in_dim | solution.py:255
  1.3 0.0 copy-start
  1.3 1.3 %copy-done = bf16[1,2,3,128,768]{4,3,2,1,0:T(8,128)(2,1)S(1)} copy-done((bf16[1,2,3,128,768]{4,3,2,1,0:T(8,128)(2,1)S(1)}, bf16[1,2,3,128,768]{4,3,2,1,0:T(8,128)(2,1)}, u32[]{:S(2)}) %copy-start) | copy-done | bytes 1179672
  2.6 0.0 copy-start.1
  2.6 1.1 %copy-done.1 = bf16[1,3,128,768]{3,2,1,0:T(8,128)(2,1)S(1)} copy-done((bf16[1,3,128,768]{3,2,1,0:T(8,128)(2,1)S(1)}, bf16[1,3,128,768]{3,2,1,0:T(8,128)(2,1)}, u32[]{:S(2)}) %copy-start.1) | copy-done | bytes 589848
  3.7 0.0 copy-start.2
  3.7 0.9 %copy-done.2 = bf16[1,128,768]{2,1,0:T(8,128)(2,1)S(1)} copy-done((bf16[1,128,768]{2,1,0:T(8,128)(2,1)S(1)}, bf16[1,128,768]{2,1,0:T(8,128)(2,1)}, u32[]{:S(2)}) %copy-start.2) | copy-done | bytes 196632
  4.6 0.0 copy-start.3
  4.6 0.7 copy-done.3
  5.2 59.6 %section_step.1 = (bf16[1,128,768]{2,1,0:T(8,128)(2,1)S(1)}, bf16[1,3,128,768]{3,2,1,0:T(8,128)(2,1)S(1)}, bf16[1,128,768]{2,1,0:T(8,128)(2,1)S(1)}) custom-call(bf16[1,3,128,768]{3,2,1,0:T(8,128)(2,1)S(1)} %copy-done.1, bf16[1,2,3,128,768]{4,3,2,1,0:T(8,128)(2,1)S(1)} %copy-done, bf16[1,128,768]{2,1,0:T(8,128)(2,1)S(1)} %copy-done.2, ...), custom_call_target="tpu_custom_call" | custom-call | tf_op jit(solution)/shard_map/section_step/pallas_call | solution.py:219
  64.9 0.7 %copy.11 = bf16[1,128,768]{2,1,0:T(8,128)(2,1)} copy(bf16[1,128,768]{2,1,0:T(8,128)(2,1)S(1)} %get-tuple-element.6) | data formatting | bytes 393216
  65.5 0.8 %copy.12 = bf16[1,3,128,768]{3,2,1,0:T(8,128)(2,1)} copy(bf16[1,3,128,768]{3,2,1,0:T(8,128)(2,1)S(1)} %get-tuple-element.7) | data formatting | bytes 1179648
  66.4 0.7 %copy.13 = bf16[1,128,768]{2,1,0:T(8,128)(2,1)} copy(bf16[1,128,768]{2,1,0:T(8,128)(2,1)S(1)} %get-tuple-element.8) | data formatting | bytes 393216
Async XLA Ops:
  1.3 1.3 %copy-start = (bf16[1,2,3,128,768]{4,3,2,1,0:T(8,128)(2,1)S(1)}, bf16[1,2,3,128,768]{4,3,2,1,0:T(8,128)(2,1)}, u32[]{:S(2)}) copy-start(bf16[1,2,3,128,768]{4,3,2,1,0:T(8,128)(2,1)} %held_ref.1) | copy-start | bytes 3538948
  2.6 1.1 %copy-start.1 = (bf16[1,3,128,768]{3,2,1,0:T(8,128)(2,1)S(1)}, bf16[1,3,128,768]{3,2,1,0:T(8,128)(2,1)}, u32[]{:S(2)}) copy-start(bf16[1,3,128,768]{3,2,1,0:T(8,128)(2,1)} %qkv_ref.1) | copy-start | bytes 1769476
  3.7 0.9 %copy-start.2 = (bf16[1,128,768]{2,1,0:T(8,128)(2,1)S(1)}, bf16[1,128,768]{2,1,0:T(8,128)(2,1)}, u32[]{:S(2)}) copy-start(bf16[1,128,768]{2,1,0:T(8,128)(2,1)} %cot_ref.1) | copy-start | bytes 589828
  4.6 0.7 copy-start.3

commit v2 on v1

--- a/solution.py
+++ b/solution.py
@@ -35,11 +35,11 @@
 
 def kernel(
     sections, members, heads, feats,
-    qkv_ref, held_ref, cot_ref, gain_ref, slot_ref,
+    qkv_ref, held_ref, cot_ref, gain_hbm, slot_hbm,
     fwd_ref, grads_ref, evict_ref,
     held_v, send_v, back_v, qkv_v, cot_v, att_v, norm_v, prob_v, pb_v, ob_v, grad_v,
     sum_v, sums_now, sums_back,
-    held_sem, qkv_sem, self_sem, zero_sem, grad_sem,
+    gain_ref, slot_ref, gain_sem, slot_sem, held_sem, qkv_sem, self_sem, zero_sem, grad_sem,
     stash_send, stash_recv, cot_send, cot_recv, evict_send, evict_recv, fwd_send, fwd_recv,
     now_send, now_recv, bsum_send, bsum_recv,
 ):
@@ -53,12 +53,16 @@
     to_self = target == p
     paired = has_up & jnp.logical_not(to_self)
 
+    slot_load = pltpu.make_async_copy(slot_hbm, slot_ref, slot_sem)
+    slot_load.start()
+    gain_load = pltpu.make_async_copy(gain_hbm, gain_ref, gain_sem)
     loads = []
     for h in range(heads):
         loads.append(pltpu.make_async_copy(held_ref.at[0, :, :, :, pl.ds(h * HS, HS)], held_v.at[h], held_sem.at[h]))
         loads[h].start()
     qkv_load = pltpu.make_async_copy(qkv_ref.at[0], qkv_v, qkv_sem)
     qkv_load.start()
+    gain_load.start()
 
     barrier = pltpu.get_barrier_semaphore()
 
@@ -101,6 +105,7 @@
             for d in range(1, members)
         ]
 
+    slot_load.wait()
     slot = slot_ref[mirror]
     for h in range(heads):
         loads[h].wait()
@@ -126,6 +131,7 @@
     rows = lax.broadcasted_iota(jnp.int32, (HS, HS), 0)
     causal = rows >= lax.broadcasted_iota(jnp.int32, (HS, HS), 1)
     qkv_load.wait()
+    gain_load.wait()
     squares = jnp.zeros((HS, HS), F32)
     for h in range(heads):
         cols = pl.ds(h * HS, HS)
@@ -146,7 +152,7 @@
     ratio = as_columns(lax.rsqrt(total / feats + EPS))
     for h in range(heads):
         cols = pl.ds(h * HS, HS)
-        norm_v[:, cols] = (att_v[:, cols].astype(F32) * ratio * gain_ref[:, cols]).astype(BF16)
+        norm_v[:, cols] = (att_v[:, cols].astype(F32) * ratio * gain_ref[cols][None, :]).astype(BF16)
     pl.when(has_up)(fwd_move.start)
 
     @pl.when(p == 0)
@@ -173,7 +179,7 @@
         ob_v[h] = out
         out = out.astype(F32)
         squares += out * out
-        dots += gain_ref[:, cols] * cot_v[:, cols].astype(F32) * out
+        dots += gain_ref[cols][None, :] * cot_v[:, cols].astype(F32) * out
     sum_v[1] = jnp.concatenate([as_row(squares), as_row(dots), jnp.zeros((6, HS), F32)], axis=0)
     back_moves = sum_moves(1, sums_back, bsum_send, bsum_recv)
     for move in back_moves:
@@ -189,7 +195,7 @@
 
     for h in range(heads):
         cols = pl.ds(h * HS, HS)
-        scaled = gain_ref[:, cols] * cot_v[:, cols].astype(F32)
+        scaled = gain_ref[cols][None, :] * cot_v[:, cols].astype(F32)
         d_out = (back_ratio * scaled - ob_v[h].astype(F32) * pull).astype(BF16)
         probs = prob_v[h]
         d_values = dot(pb_v[h], d_out, ((0,), (0,)))
@@ -211,24 +217,33 @@
     evict_move.wait()
 
 
+def hand_over(fwd_in, grads_in, evict_in, fwd_out, grads_out, evict_out, sems):
+    moves = [
+        pltpu.make_async_copy(fwd_in, fwd_out, sems.at[0]),
+        pltpu.make_async_copy(grads_in, grads_out, sems.at[1]),
+        pltpu.make_async_copy(evict_in, evict_out, sems.at[2]),
+    ]
+    for move in moves:
+        move.start()
+    for move in moves:
+        move.wait()
+
+
 def shards(sections, members, qkv_now, held_stash, cotangent, norm_gain, fetch_slot):
     rows, width = cotangent.shape[1:]
     heads = width // HS
     anywhere = pl.BlockSpec(memory_space=pl.ANY)
     dma = pltpu.SemaphoreType.DMA
-    return pl.pallas_call(
+    in_hbm = functools.partial(pltpu.with_memory_space_constraint, memory_space=pltpu.HBM)
+    results = pl.pallas_call(
         functools.partial(kernel, sections, members, heads, float(width * members)),
         name="section_step",
         out_shape=(
-            jax.ShapeDtypeStruct((1, rows, width), BF16),
-            jax.ShapeDtypeStruct((1, 3, rows, width), BF16),
-            jax.ShapeDtypeStruct((1, rows, width), BF16),
+            pltpu.VMEM((1, rows, width), BF16),
+            pltpu.VMEM((1, 3, rows, width), BF16),
+            pltpu.VMEM((1, rows, width), BF16),
         ),
-        in_specs=[
-            anywhere, anywhere, anywhere,
-            pl.BlockSpec(memory_space=pltpu.VMEM),
-            pl.BlockSpec(memory_space=pltpu.SMEM),
-        ],
+        in_specs=[anywhere] * 5,
         out_specs=(anywhere, anywhere, anywhere),
         scratch_shapes=[
             pltpu.VMEM((heads, 2, 3, rows, HS), BF16),
@@ -245,14 +260,22 @@
             pltpu.VMEM((2, 8, rows), F32),
             pltpu.VMEM((members - 1, 8, rows), F32),
             pltpu.VMEM((members - 1, 8, rows), F32),
-            dma((heads,)), dma, dma, dma, dma,
+            pltpu.VMEM((width,), F32),
+            pltpu.SMEM((sections,), jnp.int32),
+            dma, dma, dma((heads,)), dma, dma, dma, dma,
             dma((heads,)), dma((heads,)), dma, dma, dma, dma, dma, dma,
             dma((members - 1,)), dma((members - 1,)), dma((members - 1,)), dma((members - 1,)),
         ],
-        compiler_params=pltpu.CompilerParams(
-            collective_id=0, has_side_effects=True, vmem_limit_bytes=24 * 1024 * 1024
-        ),
-    )(qkv_now, held_stash, cotangent, norm_gain[None, :], fetch_slot)
+        compiler_params=pltpu.CompilerParams(collective_id=0, has_side_effects=True, vmem_limit_bytes=24 * 1024 * 1024),
+    )(in_hbm(qkv_now), in_hbm(held_stash), in_hbm(cotangent), in_hbm(norm_gain), in_hbm(fetch_slot))
+    return pl.pallas_call(
+        hand_over,
+        name="hand_over",
+        out_shape=tuple(pltpu.HBM(r.shape, r.dtype) for r in results),
+        in_specs=[pl.BlockSpec(memory_space=pltpu.VMEM)] * 3,
+        out_specs=(anywhere,) * 3,
+        scratch_shapes=[dma((3,))],
+    )(*[pltpu.with_memory_space_constraint(r, memory_space=pltpu.VMEM) for r in results])
 
 
 def solution(mesh):

time: 67.3 us -> 60.4 us (0.90)
  local copies, waits for them, and re-layouts: 6.78 us -> 0 us
    unnamed x11 -> x0, local copies, waits for them, and re-layouts: 6.08 us -> none
    pallas_call x1, Pallas kernels: 59.6 us -> 58.6 us  [shards(): pl.pallas_call(functools.partial(kernel, sections, members, heads, float(...]
    pallas_call x0 -> x1, Pallas kernels: none -> 0.96 us  [shards(): pl.pallas_call(hand_over, name='hand_over', out_shape=tuple((pltpu.HBM(r....]
    broadcast_in_dim x1 -> x0, local copies, waits for them, and re-layouts: 0.69 us -> none  [shards(): norm_gain[None, :]]
where the time goes in v2:
time: 60.4 us; the launch traced here: 60.3 us
  Pallas kernels  59.6 us (99%)
  between operations  0.64 us (1%)
    pallas_call x1, Pallas kernels, shards(): pl.pallas_call(functools.partial(kernel, sections, members, heads, float(...  58.6 us

profile of v2, /device:TPU:57, one launch (start us, length us, event | category | flops | bytes accessed | tf_op | source)
XLA Modules:
  0.0 60.3 jit_solution(10660822898961736560)
XLA Ops:
  0.6 58.6 %section_step.1 = (bf16[1,128,768]{2,1,0:T(8,128)(2,1)S(1)}, bf16[1,3,128,768]{3,2,1,0:T(8,128)(2,1)S(1)}, bf16[1,128,768]{2,1,0:T(8,128)(2,1)S(1)}) custom-call(bf16[1,3,128,768]{3,2,1,0:T(8,128)(2,1)} %qkv_ref.1, bf16[1,2,3,128,768]{4,3,2,1,0:T(8,128)(2,1)} %held_ref.1, bf16[1,128,768]{2,1,0:T(8,128)(2,1)} %cot_ref.1, f32[768]{0:T(1024)} %gain_hbm.1, ...), custom_call_target="tpu_custom_call" | custom-call | tf_op jit(solution)/shard_map/section_step/pallas_call | solution.py:238
  59.3 1.0 %hand_over.1 = (bf16[1,128,768]{2,1,0:T(8,128)(2,1)}, bf16[1,3,128,768]{3,2,1,0:T(8,128)(2,1)}, bf16[1,128,768]{2,1,0:T(8,128)(2,1)}) custom-call(bf16[1,128,768]{2,1,0:T(8,128)(2,1)S(1)} %get-tuple-element.6.fwd_in, bf16[1,3,128,768]{3,2,1,0:T(8,128)(2,1)S(1)} %get-tuple-element.7.grads_in, bf16[1,128,768]{2,1,0:T(8,128)(2,1)S(1)} %get-tuple-element.8.evict_in), custom_call_target="tpu_custom_call" | custom-call | tf_op jit(solution)/shard_map/hand_over/pallas_call | solution.py:271

commit v3 on v2

--- a/solution.py
+++ b/solution.py
@@ -37,11 +37,11 @@
     sections, members, heads, feats,
     qkv_ref, held_ref, cot_ref, gain_hbm, slot_hbm,
     fwd_ref, grads_ref, evict_ref,
-    held_v, send_v, back_v, qkv_v, cot_v, att_v, norm_v, prob_v, pb_v, ob_v, grad_v,
+    held_v, send_v, back_v, qkv_v, cot_v, att_v, norm_v, prob_v, pb_v, ob_v, grad_v, part_v,
     sum_v, sums_now, sums_back,
     gain_ref, slot_ref, gain_sem, slot_sem, held_sem, qkv_sem, self_sem, zero_sem, grad_sem,
     stash_send, stash_recv, cot_send, cot_recv, evict_send, evict_recv, fwd_send, fwd_recv,
-    now_send, now_recv, bsum_send, bsum_recv,
+    now_send, now_recv, bsum_send, bsum_recv, up_ready, down_ready,
 ):
     p = lax.axis_index("pipe")
     t = lax.axis_index("tensor")
@@ -51,6 +51,12 @@
     has_up = p < last
     has_down = p > 0
     to_self = target == p
+    late = p >= sections // 2
+    early = jnp.logical_not(late)
+    core = lax.rem(p, 2)
+    yh = lax.rem(p, 8) // 2
+    at_once = late & (core == 1) & (yh == 1)
+    behind = late & jnp.logical_not(at_once)
     paired = has_up & jnp.logical_not(to_self)
 
     slot_load = pltpu.make_async_copy(slot_hbm, slot_ref, slot_sem)
@@ -71,8 +77,6 @@
 
     greet(mirror, t)
     pl.when(paired)(lambda: greet(target, t))
-    pl.when(has_up)(lambda: greet(p + 1, t))
-    pl.when(has_down)(lambda: greet(p - 1, t))
     for d in range(1, members):
         greet(p, lax.rem(t + d, members))
 
@@ -105,28 +109,25 @@
             for d in range(1, members)
         ]
 
-    slot_load.wait()
-    slot = slot_ref[mirror]
-    for h in range(heads):
+    def choose(h):
         loads[h].wait()
         for i in range(3):
             send_v[h, i] = jnp.where(slot == 1, held_v[h, 1, i], held_v[h, 0, i])
-        if h == 0:
-            pl.semaphore_wait(barrier, members + one(paired) + one(has_up) + one(has_down))
+
+    slot_load.wait()
+    slot = slot_ref[mirror]
+    for h in range(1):
+        choose(h)
+    pl.semaphore_wait(barrier, members + one(paired))
+
+    for h in range(1):
         pl.when(paired)(stash[h].start)
 
-    pl.when(has_down)(cot_move.start)
-
-    @pl.when(to_self)
-    def _():
-        own = pltpu.make_async_copy(send_v, back_v, self_sem)
-        own.start()
-        own.wait()
-
-    @pl.when(p == last)
-    def _():
-        back_v[...] = jnp.zeros_like(back_v)
-        cot_v[...] = jnp.zeros_like(cot_v)
+    def vouch(sem, section):
+        pl.semaphore_signal(sem, inc=1, device_id=(section, t), device_id_type=MESH)
+
+    pl.when(has_up)(lambda: vouch(down_ready, mirror))
+    pl.when(paired)(lambda: vouch(up_ready, target))
 
     rows = lax.broadcasted_iota(jnp.int32, (HS, HS), 0)
     causal = rows >= lax.broadcasted_iota(jnp.int32, (HS, HS), 1)
@@ -144,6 +145,25 @@
     now_moves = sum_moves(0, sums_now, now_send, now_recv)
     for move in now_moves:
         move.start()
+    for h in range(1, heads):
+        choose(h)
+        pl.when(paired)(stash[h].start)
+
+    pl.when(at_once)(evict_move.start)
+    pl.when(has_down)(lambda: pl.semaphore_wait(down_ready, 1))
+    pl.when(has_down)(cot_move.start)
+
+    @pl.when(to_self)
+    def _():
+        own = pltpu.make_async_copy(send_v, back_v, self_sem)
+        own.start()
+        own.wait()
+
+    @pl.when(p == last)
+    def _():
+        back_v[...] = jnp.zeros_like(back_v)
+        cot_v[...] = jnp.zeros_like(cot_v)
+
     for move in now_moves:
         move.wait_recv()
     total = sum_v[0, 0:1]
@@ -153,6 +173,7 @@
     for h in range(heads):
         cols = pl.ds(h * HS, HS)
         norm_v[:, cols] = (att_v[:, cols].astype(F32) * ratio * gain_ref[cols][None, :]).astype(BF16)
+    pl.when(paired)(lambda: pl.semaphore_wait(up_ready, 1))
     pl.when(has_up)(fwd_move.start)
 
     @pl.when(p == 0)
@@ -162,14 +183,32 @@
         zeros.start()
         zeros.wait()
 
+    def scaled_cot(h):
+        cols = pl.ds(h * HS, HS)
+        return gain_ref[cols][None, :] * cot_v[:, cols].astype(F32)
+
+    def prepare(h):
+        probs = prob_v[h]
+        rest = scaled_cot(h)
+        d_probs = jnp.zeros((HS, HS), F32)
+        for _ in range(3):
+            piece = rest.astype(BF16)
+            rest = rest - piece.astype(F32)
+            d_probs += dot(piece, back_v[h, 2], ((1,), (1,)))
+        part_v[h, 0] = probs * (d_probs - jnp.sum(probs * d_probs, axis=-1, keepdims=True)) * HS ** (-0.5)
+        d_probs = dot(ob_v[h], back_v[h, 2], ((1,), (1,)))
+        part_v[h, 1] = probs * (d_probs - jnp.sum(probs * d_probs, axis=-1, keepdims=True)) * HS ** (-0.5)
+
     pl.when(has_up)(cot_move.wait_recv)
     squares = jnp.zeros((HS, HS), F32)
     dots = jnp.zeros((HS, HS), F32)
     for h in range(heads):
         cols = pl.ds(h * HS, HS)
-        pl.when(paired)(stash[h].wait_send)
         if h == heads - 1:
-            evict_move.start()
+            for move in stash:
+                pl.when(paired & behind)(move.wait_send)
+        if h == heads - 1:
+            pl.when(behind)(evict_move.start)
         pl.when(paired)(stash[h].wait_recv)
         probs = softmax_rows(back_v[h, 0], back_v[h, 1], causal)
         prob_v[h] = probs
@@ -179,11 +218,15 @@
         ob_v[h] = out
         out = out.astype(F32)
         squares += out * out
-        dots += gain_ref[cols][None, :] * cot_v[:, cols].astype(F32) * out
+        dots += scaled_cot(h) * out
+        if h < heads - 1:
+            prepare(h)
     sum_v[1] = jnp.concatenate([as_row(squares), as_row(dots), jnp.zeros((6, HS), F32)], axis=0)
     back_moves = sum_moves(1, sums_back, bsum_send, bsum_recv)
     for move in back_moves:
         move.start()
+    pl.when(early)(evict_move.start)
+    prepare(heads - 1)
     for move in back_moves:
         move.wait_recv()
     total = sum_v[1]
@@ -193,27 +236,26 @@
     pull = as_columns(back_ratio**3 * total[1:2] / feats)
     back_ratio = as_columns(back_ratio)
 
-    for h in range(heads):
-        cols = pl.ds(h * HS, HS)
-        scaled = gain_ref[cols][None, :] * cot_v[:, cols].astype(F32)
-        d_out = (back_ratio * scaled - ob_v[h].astype(F32) * pull).astype(BF16)
-        probs = prob_v[h]
-        d_values = dot(pb_v[h], d_out, ((0,), (0,)))
-        d_probs = dot(d_out, back_v[h, 2], ((1,), (1,)))
-        delta = jnp.sum(probs * d_probs, axis=-1, keepdims=True)
-        d_scores = (probs * (d_probs - delta) * HS ** (-0.5)).astype(BF16)
+    grad_moves = []
+    for h in range(heads):
+        cols = pl.ds(h * HS, HS)
+        d_out = (back_ratio * scaled_cot(h) - ob_v[h].astype(F32) * pull).astype(BF16)
+        d_scores = (back_ratio * part_v[h, 0] - pull * part_v[h, 1]).astype(BF16)
         grad_v[0, :, cols] = dot(d_scores, back_v[h, 1], ((1,), (0,))).astype(BF16)
         grad_v[1, :, cols] = dot(d_scores, back_v[h, 0], ((0,), (0,))).astype(BF16)
-        grad_v[2, :, cols] = d_values.astype(BF16)
-    grads_out = pltpu.make_async_copy(grad_v, grads_ref.at[0], grad_sem)
-    grads_out.start()
+        grad_v[2, :, cols] = dot(pb_v[h], d_out, ((0,), (0,))).astype(BF16)
+        grad_moves.append(pltpu.make_async_copy(grad_v.at[:, :, cols], grads_ref.at[0, :, :, cols], grad_sem.at[h]))
+        grad_moves[h].start()
 
     pl.when(has_down)(cot_move.wait_send)
     pl.when(has_up)(fwd_move.wait_send)
     pl.when(has_down)(fwd_move.wait_recv)
     for move in now_moves + back_moves:
         move.wait_send()
-    grads_out.wait()
+    for move in stash:
+        pl.when(paired & jnp.logical_not(behind))(move.wait_send)
+    for move in grad_moves:
+        move.wait()
     evict_move.wait()
 
 
@@ -257,14 +299,16 @@
             pltpu.VMEM((heads, rows, rows), BF16),
             pltpu.VMEM((heads, rows, HS), BF16),
             pltpu.VMEM((3, rows, width), BF16),
+            pltpu.VMEM((heads, 2, rows, rows), F32),
             pltpu.VMEM((2, 8, rows), F32),
             pltpu.VMEM((members - 1, 8, rows), F32),
             pltpu.VMEM((members - 1, 8, rows), F32),
             pltpu.VMEM((width,), F32),
             pltpu.SMEM((sections,), jnp.int32),
-            dma, dma, dma((heads,)), dma, dma, dma, dma,
+            dma, dma, dma((heads,)), dma, dma, dma, dma((heads,)),
             dma((heads,)), dma((heads,)), dma, dma, dma, dma, dma, dma,
             dma((members - 1,)), dma((members - 1,)), dma((members - 1,)), dma((members - 1,)),
+            pltpu.SemaphoreType.REGULAR, pltpu.SemaphoreType.REGULAR,
         ],
         compiler_params=pltpu.CompilerParams(collective_id=0, has_side_effects=True, vmem_limit_bytes=24 * 1024 * 1024),
     )(in_hbm(qkv_now), in_hbm(held_stash), in_hbm(cotangent), in_hbm(norm_gain), in_hbm(fetch_slot))

time: 60.4 us -> 57.4 us (0.950)
  Pallas kernels: 59.6 us -> 56.6 us
    pallas_call x1, Pallas kernels: 58.6 us -> 55.6 us  [shards(): pl.pallas_call(functools.partial(kernel, sections, members, heads, float(...]
where the time goes in v3:
time: 57.4 us; the launch traced here: 57.2 us
  Pallas kernels  56.6 us (99%)
  between operations  0.64 us (1%)
    pallas_call x1, Pallas kernels, shards(): pl.pallas_call(functools.partial(kernel, sections, members, heads, float(...  55.6 us

profile of v3, /device:TPU:57, one launch (start us, length us, event | category | flops | bytes accessed | tf_op | source)
XLA Modules:
  0.0 57.2 jit_solution(11102292669402875560)
XLA Ops:
  0.6 55.6 %section_step.1 = (bf16[1,128,768]{2,1,0:T(8,128)(2,1)S(1)}, bf16[1,3,128,768]{3,2,1,0:T(8,128)(2,1)S(1)}, bf16[1,128,768]{2,1,0:T(8,128)(2,1)S(1)}) custom-call(bf16[1,3,128,768]{3,2,1,0:T(8,128)(2,1)} %qkv_ref.1, bf16[1,2,3,128,768]{4,3,2,1,0:T(8,128)(2,1)} %held_ref.1, bf16[1,128,768]{2,1,0:T(8,128)(2,1)} %cot_ref.1, f32[768]{0:T(1024)} %gain_hbm.1, ...), custom_call_target="tpu_custom_call" | custom-call | tf_op jit(solution)/shard_map/section_step/pallas_call | solution.py:280
  56.3 1.0 %hand_over.1 = (bf16[1,128,768]{2,1,0:T(8,128)(2,1)}, bf16[1,3,128,768]{3,2,1,0:T(8,128)(2,1)}, bf16[1,128,768]{2,1,0:T(8,128)(2,1)}) custom-call(bf16[1,128,768]{2,1,0:T(8,128)(2,1)S(1)} %get-tuple-element.6.fwd_in, bf16[1,3,128,768]{3,2,1,0:T(8,128)(2,1)S(1)} %get-tuple-element.7.grads_in, bf16[1,128,768]{2,1,0:T(8,128)(2,1)S(1)} %get-tuple-element.8.evict_in), custom_call_target="tpu_custom_call" | custom-call | tf_op jit(solution)/shard_map/hand_over/pallas_call | solution.py:315

commit v4 on v3

--- a/solution.py
+++ b/solution.py
@@ -146,12 +146,13 @@
     for move in now_moves:
         move.start()
     for h in range(1, heads):
+        if h == 4:
+            pl.when(has_down)(lambda: pl.semaphore_wait(down_ready, 1))
+            pl.when(has_down)(cot_move.start)
         choose(h)
         pl.when(paired)(stash[h].start)
 
     pl.when(at_once)(evict_move.start)
-    pl.when(has_down)(lambda: pl.semaphore_wait(down_ready, 1))
-    pl.when(has_down)(cot_move.start)
 
     @pl.when(to_self)
     def _():
@@ -225,7 +226,7 @@
     back_moves = sum_moves(1, sums_back, bsum_send, bsum_recv)
     for move in back_moves:
         move.start()
-    pl.when(early)(evict_move.start)
+    pl.when(jnp.logical_not(at_once | behind))(evict_move.start)
     prepare(heads - 1)
     for move in back_moves:
         move.wait_recv()

time: 57.4 us -> 55 us (0.958)
  the two profiles are of different devices: /device:TPU:57 before, /device:TPU:81 now
where the time goes in v4:
time: 55 us; the launch traced here: 54.8 us
  Pallas kernels  54.2 us (99%)
  between operations  0.64 us (1%)
    pallas_call x1, Pallas kernels, shards(): pl.pallas_call(functools.partial(kernel, sections, members, heads, float(...  53.2 us

profile of v4, /device:TPU:81, one launch (start us, length us, event | category | flops | bytes accessed | tf_op | source)
XLA Modules:
  0.0 54.8 jit_solution(3993086810208952672)
XLA Ops:
  0.6 53.2 %section_step.1 = (bf16[1,128,768]{2,1,0:T(8,128)(2,1)S(1)}, bf16[1,3,128,768]{3,2,1,0:T(8,128)(2,1)S(1)}, bf16[1,128,768]{2,1,0:T(8,128)(2,1)S(1)}) custom-call(bf16[1,3,128,768]{3,2,1,0:T(8,128)(2,1)} %qkv_ref.1, bf16[1,2,3,128,768]{4,3,2,1,0:T(8,128)(2,1)} %held_ref.1, bf16[1,128,768]{2,1,0:T(8,128)(2,1)} %cot_ref.1, f32[768]{0:T(1024)} %gain_hbm.1, ...), custom_call_target="tpu_custom_call" | custom-call | tf_op jit(solution)/shard_map/section_step/pallas_call | solution.py:281
  53.9 1.0 %hand_over.1 = (bf16[1,128,768]{2,1,0:T(8,128)(2,1)}, bf16[1,3,128,768]{3,2,1,0:T(8,128)(2,1)}, bf16[1,128,768]{2,1,0:T(8,128)(2,1)}) custom-call(bf16[1,128,768]{2,1,0:T(8,128)(2,1)S(1)} %get-tuple-element.6.fwd_in, bf16[1,3,128,768]{3,2,1,0:T(8,128)(2,1)S(1)} %get-tuple-element.7.grads_in, bf16[1,128,768]{2,1,0:T(8,128)(2,1)S(1)} %get-tuple-element.8.evict_in), custom_call_target="tpu_custom_call" | custom-call | tf_op jit(solution)/shard_map/hand_over/pallas_call | solution.py:316

commit v5 on v4

--- a/solution.py
+++ b/solution.py
@@ -55,7 +55,7 @@
     early = jnp.logical_not(late)
     core = lax.rem(p, 2)
     yh = lax.rem(p, 8) // 2
-    at_once = late & (core == 1) & (yh == 1)
+    at_once = late & (((core == 1) & (yh == 1)) | ((core == 0) & (yh == 3) & (p // 8 == 5)))
     behind = late & jnp.logical_not(at_once)
     paired = has_up & jnp.logical_not(to_self)
 
@@ -118,16 +118,17 @@
     slot = slot_ref[mirror]
     for h in range(1):
         choose(h)
-    pl.semaphore_wait(barrier, members + one(paired))
-
-    for h in range(1):
-        pl.when(paired)(stash[h].start)
+    def enter():
+        pl.semaphore_wait(barrier, members + one(paired))
+        for h in range(1):
+            pl.when(paired)(stash[h].start)
+        pl.when(has_up)(lambda: vouch(down_ready, mirror))
+        pl.when(paired)(lambda: vouch(up_ready, target))
 
     def vouch(sem, section):
         pl.semaphore_signal(sem, inc=1, device_id=(section, t), device_id_type=MESH)
 
-    pl.when(has_up)(lambda: vouch(down_ready, mirror))
-    pl.when(paired)(lambda: vouch(up_ready, target))
+    pl.when(late)(enter)
 
     rows = lax.broadcasted_iota(jnp.int32, (HS, HS), 0)
     causal = rows >= lax.broadcasted_iota(jnp.int32, (HS, HS), 1)
@@ -142,11 +143,12 @@
         out = out.astype(F32)
         squares += out * out
     sum_v[0] = jnp.broadcast_to(as_row(squares), (8, HS))
+    pl.when(early)(enter)
     now_moves = sum_moves(0, sums_now, now_send, now_recv)
     for move in now_moves:
         move.start()
     for h in range(1, heads):
-        if h == 4:
+        if h == 3:
             pl.when(has_down)(lambda: pl.semaphore_wait(down_ready, 1))
             pl.when(has_down)(cot_move.start)
         choose(h)

time: 55 us -> 54.2 us (0.985)
  the two profiles are of different devices: /device:TPU:81 before, /device:TPU:16 now
where the time goes in v5:
time: 54.2 us; the launch traced here: 54 us
  Pallas kernels  53.4 us (99%)
  between operations  0.64 us (1%)
    pallas_call x1, Pallas kernels, shards(): pl.pallas_call(functools.partial(kernel, sections, members, heads, float(...  52.4 us

profile of v5, /device:TPU:16, one launch (start us, length us, event | category | flops | bytes accessed | tf_op | source)
XLA Modules:
  0.0 54.0 jit_solution(13385789847754658984)
XLA Ops:
  0.6 52.4 %section_step.1 = (bf16[1,128,768]{2,1,0:T(8,128)(2,1)S(1)}, bf16[1,3,128,768]{3,2,1,0:T(8,128)(2,1)S(1)}, bf16[1,128,768]{2,1,0:T(8,128)(2,1)S(1)}) custom-call(bf16[1,3,128,768]{3,2,1,0:T(8,128)(2,1)} %qkv_ref.1, bf16[1,2,3,128,768]{4,3,2,1,0:T(8,128)(2,1)} %held_ref.1, bf16[1,128,768]{2,1,0:T(8,128)(2,1)} %cot_ref.1, f32[768]{0:T(1024)} %gain_hbm.1, ...), custom_call_target="tpu_custom_call" | custom-call | tf_op jit(solution)/shard_map/section_step/pallas_call | solution.py:283
  53.0 1.0 %hand_over.1 = (bf16[1,128,768]{2,1,0:T(8,128)(2,1)}, bf16[1,3,128,768]{3,2,1,0:T(8,128)(2,1)}, bf16[1,128,768]{2,1,0:T(8,128)(2,1)}) custom-call(bf16[1,128,768]{2,1,0:T(8,128)(2,1)S(1)} %get-tuple-element.6.fwd_in, bf16[1,3,128,768]{3,2,1,0:T(8,128)(2,1)S(1)} %get-tuple-element.7.grads_in, bf16[1,128,768]{2,1,0:T(8,128)(2,1)S(1)} %get-tuple-element.8.evict_in), custom_call_target="tpu_custom_call" | custom-call | tf_op jit(solution)/shard_map/hand_over/pallas_call | solution.py:318

commit v6 on v5

--- a/solution.py
+++ b/solution.py
@@ -55,8 +55,8 @@
     early = jnp.logical_not(late)
     core = lax.rem(p, 2)
     yh = lax.rem(p, 8) // 2
-    at_once = late & (((core == 1) & (yh == 1)) | ((core == 0) & (yh == 3) & (p // 8 == 5)))
-    behind = late & jnp.logical_not(at_once)
+    at_once = late & (((core == 1) & (yh == 1)) | ((core == 0) & (yh == 3) & (p // 8 == 5)) | ((core == 0) & (yh == 2) & (p // 8 == 6)))
+    behind = late & jnp.logical_not(at_once) & jnp.logical_not((core == 1) & (yh == 2))
     paired = has_up & jnp.logical_not(to_self)
 
     slot_load = pltpu.make_async_copy(slot_hbm, slot_ref, slot_sem)
@@ -147,14 +147,12 @@
     now_moves = sum_moves(0, sums_now, now_send, now_recv)
     for move in now_moves:
         move.start()
+    window = 2
     for h in range(1, heads):
-        if h == 3:
-            pl.when(has_down)(lambda: pl.semaphore_wait(down_ready, 1))
-            pl.when(has_down)(cot_move.start)
         choose(h)
+    for h in range(1, window):
         pl.when(paired)(stash[h].start)
 
-    pl.when(at_once)(evict_move.start)
 
     @pl.when(to_self)
     def _():
@@ -185,6 +183,14 @@
         zeros = pltpu.make_async_copy(grad_v.at[0], fwd_ref.at[0], zero_sem)
         zeros.start()
         zeros.wait()
+
+    for h in range(window, heads):
+        if h == 3:
+            pl.when(has_down)(lambda: pl.semaphore_wait(down_ready, 1))
+            pl.when(has_down)(cot_move.start)
+        pl.when(paired)(stash[h - window].wait_send)
+        pl.when(paired)(stash[h].start)
+    pl.when(at_once)(evict_move.start)
 
     def scaled_cot(h):
         cols = pl.ds(h * HS, HS)
@@ -208,7 +214,7 @@
     for h in range(heads):
         cols = pl.ds(h * HS, HS)
         if h == heads - 1:
-            for move in stash:
+            for move in stash[heads - window:]:
                 pl.when(paired & behind)(move.wait_send)
         if h == heads - 1:
             pl.when(behind)(evict_move.start)
@@ -255,7 +261,7 @@
     pl.when(has_down)(fwd_move.wait_recv)
     for move in now_moves + back_moves:
         move.wait_send()
-    for move in stash:
+    for move in stash[heads - window:]:
         pl.when(paired & jnp.logical_not(behind))(move.wait_send)
     for move in grad_moves:
         move.wait()

time: 54.2 us -> 54.4 us (level)
  the two profiles are of different devices: /device:TPU:16 before, /device:TPU:17 now
where the time goes in v6:
time: 54.4 us; the launch traced here: 54.3 us
  Pallas kernels  53.6 us (99%)
  between operations  0.64 us (1%)
    pallas_call x1, Pallas kernels, shards(): pl.pallas_call(functools.partial(kernel, sections, members, heads, float(...  52.7 us

profile of v6, /device:TPU:17, one launch (start us, length us, event | category | flops | bytes accessed | tf_op | source)
XLA Modules:
  0.0 54.3 jit_solution(4398774495198471650)
XLA Ops:
  0.6 52.7 %section_step.1 = (bf16[1,128,768]{2,1,0:T(8,128)(2,1)S(1)}, bf16[1,3,128,768]{3,2,1,0:T(8,128)(2,1)S(1)}, bf16[1,128,768]{2,1,0:T(8,128)(2,1)S(1)}) custom-call(bf16[1,3,128,768]{3,2,1,0:T(8,128)(2,1)} %qkv_ref.1, bf16[1,2,3,128,768]{4,3,2,1,0:T(8,128)(2,1)} %held_ref.1, bf16[1,128,768]{2,1,0:T(8,128)(2,1)} %cot_ref.1, f32[768]{0:T(1024)} %gain_hbm.1, ...), custom_call_target="tpu_custom_call" | custom-call | tf_op jit(solution)/shard_map/section_step/pallas_call | solution.py:289
  53.3 1.0 %hand_over.1 = (bf16[1,128,768]{2,1,0:T(8,128)(2,1)}, bf16[1,3,128,768]{3,2,1,0:T(8,128)(2,1)}, bf16[1,128,768]{2,1,0:T(8,128)(2,1)}) custom-call(bf16[1,128,768]{2,1,0:T(8,128)(2,1)S(1)} %get-tuple-element.6.fwd_in, bf16[1,3,128,768]{3,2,1,0:T(8,128)(2,1)S(1)} %get-tuple-element.7.grads_in, bf16[1,128,768]{2,1,0:T(8,128)(2,1)S(1)} %get-tuple-element.8.evict_in), custom_call_target="tpu_custom_call" | custom-call | tf_op jit(solution)/shard_map/hand_over/pallas_call | solution.py:324
